TPU v7x, 256 devices: a whole 4x4x8 slice. The times are simulated.
256 devices in a mesh: tm: 4 (over x), space: 64 (over z, y, core).
Axes of the slice: x: 4, y: 4, z: 8, core: 2. Of those that a mesh axis runs over, the one named last changes fastest.
Arguments:
- flow_state: float32 [16, 6, 128, 32, 128], P('tm', None, 'space'), may hold values from -0.65 to 3.75, as said below
- metrics: float32 [11, 128, 32, 128], P(None, 'space', 'tm'), may hold values from -0.3 to 2, as said below
Outputs:
- increment: float32 [16, 6, 128, 32, 128], P('tm', None, 'space')
Inputs may be any that keep to these rules, and one draw needn't show every extreme that they name: `flow_state`: physical conserved states: density between 0.7 and 1.3, speed components below 0.5 in magnitude, pressure between 0.7 and 1.3, turbulent viscosity between 0.01 and 0.1. `metrics`: face vectors have a leading component between 0.7 and 1.3 along their own dimension and others of at most 0.3; volumes lie between 0.6 and 1.6, wall distances between 0.2 and 2.
All inputs are finite; a program needn't handle non-finite values.
Results may differ from a plain program's by a relative error of at most 0.00023.
Values sent between devices are 32-bit elements; how exact they have to be, the bound alone decides.
A program may use at most 64 MiB of HBM per device.

v0:
```python
import math

import jax
import jax.numpy as jnp
import numpy as np
from jax import lax
from jax.sharding import PartitionSpec as P

NINST = 16
SECTIONS = 2


GAMMA = 1.4
EPS_TWO = 0.1
EPS_FOUR = 0.03125
VISCOSITY = 0.02
HEAT_FACTOR = 1.4 / (0.4 * 0.72)
TURB_DIFFUSE = 1.5
WALL_COEFF = 3.24
OMEGA = 1.0
CFL_NUMBER = 0.5


def with_halo(shard, sides, width):
    for axis, dim in sides:
        size, length = (lax.axis_size(axis), shard.shape[dim])
        up = [(i, (i + 1) % size) for i in range(size)]
        down = [(j, i) for i, j in up]
        last = lax.slice_in_dim(shard, length - width, length, axis=dim)
        leading = lax.slice_in_dim(shard, 0, width, axis=dim)
        before = lax.ppermute(last, axis, up)
        after = lax.ppermute(leading, axis, down)
        shard = jnp.concatenate([before, shard, after], axis=dim)
    return shard


def spectral_table(length):
    table_rows = []
    for first in range(length):
        entries = []
        for second in range(length):
            offset = first - second
            if offset == 0:
                entries.append(0.0)
            else:
                parity = 1.0 if offset % 2 == 0 else -1.0
                entries.append(0.5 * parity / math.tan(math.pi * offset / length))
        table_rows.append(entries)
    return np.array(table_rows)


def primitives(states):
    density = states[:, 0]
    velocity = states[:, 1:4] / density[:, None]
    pressure = (GAMMA - 1.0) * (states[:, 4] - 0.5 * jnp.sum(states[:, 1:4] * velocity, axis=1))
    return (density, velocity, pressure)


def convective(states, velocity, pressure, normal):
    normal_flow = jnp.sum(velocity * normal[None], axis=1)
    mass_flux = states[:, 0] * normal_flow
    momentum_flux = states[:, 1:4] * normal_flow[:, None] + pressure[:, None] * normal[None]
    energy_flux = (states[:, 4] + pressure) * normal_flow
    turbulent_flux = states[:, 5] * normal_flow
    return jnp.concatenate(
        [mass_flux[:, None], momentum_flux, energy_flux[:, None], turbulent_flux[:, None]], axis=1
    )


def spectral_radius(left_cells, right_cells, normal):
    left_rho, left_vel, left_pre = primitives(left_cells)
    right_rho, right_vel, right_pre = primitives(right_cells)
    normal_flow = 0.5 * jnp.sum((left_vel + right_vel) * normal[None], axis=1)
    sound_speed = 0.5 * (
        jnp.sqrt(GAMMA * left_pre / left_rho) + jnp.sqrt(GAMMA * right_pre / right_rho)
    )
    return jnp.abs(normal_flow) + sound_speed * jnp.sqrt(jnp.sum(normal * normal, axis=0))[None]


def face_flux(
    outer_left, left_cells, right_cells, outer_right, normal, left_volume, right_volume, radius
):
    left_rho, left_vel, left_pre = primitives(left_cells)
    right_rho, right_vel, right_pre = primitives(right_cells)
    central = 0.5 * (
        convective(left_cells, left_vel, left_pre, normal)
        + convective(right_cells, right_vel, right_pre, normal)
    )
    jump_one = right_cells - left_cells
    jump_three = outer_right - 3.0 * right_cells + 3.0 * left_cells - outer_left
    damping = radius[:, None] * (EPS_TWO * jump_one - EPS_FOUR * jump_three)
    mu_face = VISCOSITY + 0.5 * (left_cells[:, 5] + right_cells[:, 5])
    conduct = (
        mu_face * (jnp.sum(normal * normal, axis=0) / (0.5 * (left_volume + right_volume)))[None]
    )
    kinetic_jump = 0.5 * (
        jnp.sum(right_vel * right_vel, axis=1) - jnp.sum(left_vel * left_vel, axis=1)
    )
    heat_jump = HEAT_FACTOR * (right_pre / right_rho - left_pre / left_rho)
    turb_jump = TURB_DIFFUSE * (right_cells[:, 5] / right_rho - left_cells[:, 5] / left_rho)
    viscous = jnp.concatenate(
        [
            jnp.zeros_like(kinetic_jump)[:, None],
            right_vel - left_vel,
            (kinetic_jump + heat_jump)[:, None],
            turb_jump[:, None],
        ],
        axis=1,
    )
    return central - damping - conduct[:, None] * viscous


def source_terms(states, distance, volume):
    destroy = (
        WALL_COEFF
        * volume[None]
        * states[:, 5]
        * states[:, 5]
        / (states[:, 0] * (distance * distance)[None])
    )
    blank_terms = jnp.zeros(states.shape[:1] + (5,) + states.shape[2:], jnp.float32)
    return jnp.concatenate([blank_terms, destroy[:, None]], axis=1)


def per_device(flow_state, metrics):
    time_table = jnp.asarray(spectral_table(NINST)).astype(jnp.float32)
    planes = flow_state.shape[2]
    assembled = lax.all_gather(metrics, "tm", axis=2, tiled=True)
    rimmed = with_halo(assembled, (("space", 1),), 1)
    own_metrics = rimmed[:, 1 : planes + 1]
    volume = own_metrics[9]
    axial_normal = rimmed[0:3, 0 : planes + 1]
    axial_left_vol = rimmed[9, 0 : planes + 1]
    axial_right_vol = rimmed[9, 1 : planes + 2]

    def widen(current):
        return with_halo(current, (("space", 2),), 2)

    widened = widen(flow_state)
    axial_radius = spectral_radius(
        widened[:, :, 1 : planes + 2], widened[:, :, 2 : planes + 3], axial_normal
    )
    denominator = OMEGA * 0.5 * NINST * volume[None] + axial_radius[:, 1:] + axial_radius[:, :-1]
    cross_radii = []
    for direction in (1, 2):
        radius = spectral_radius(
            flow_state,
            jnp.roll(flow_state, -1, direction + 2),
            own_metrics[3 * direction : 3 * direction + 3],
        )
        cross_radii.append(radius)
        denominator = denominator + radius + jnp.roll(radius, 1, direction + 1)
    pseudo_step = CFL_NUMBER / denominator
    current = flow_state
    for section_index in range(SECTIONS):
        if section_index > 0:
            widened = widen(current)
        block = lax.all_to_all(current, "tm", split_axis=3, concat_axis=0, tiled=True)
        block_shape = block.shape
        mixed = jnp.dot(
            time_table, block.reshape(block_shape[0], -1), precision=lax.Precision.HIGHEST
        ).reshape(block_shape)
        coupled = lax.all_to_all(mixed, "tm", split_axis=0, concat_axis=3, tiled=True)
        axial_terms = face_flux(
            widened[:, :, 0 : planes + 1],
            widened[:, :, 1 : planes + 2],
            widened[:, :, 2 : planes + 3],
            widened[:, :, 3 : planes + 4],
            axial_normal,
            axial_left_vol,
            axial_right_vol,
            axial_radius,
        )
        summed = (
            source_terms(current, own_metrics[10], volume)
            + axial_terms[:, :, 1:]
            - axial_terms[:, :, :-1]
        )
        for direction in (1, 2):
            axis_state = direction + 2
            face_terms = face_flux(
                jnp.roll(current, 1, axis_state),
                current,
                jnp.roll(current, -1, axis_state),
                jnp.roll(current, -2, axis_state),
                own_metrics[3 * direction : 3 * direction + 3],
                volume,
                jnp.roll(volume, -1, direction),
                cross_radii[direction - 1],
            )
            summed = summed + face_terms - jnp.roll(face_terms, 1, axis_state)
        summed = summed + OMEGA * volume[None] * coupled
        current = flow_state - 1.0 / (SECTIONS - section_index) * pseudo_step[:, None] * summed
    return current - flow_state


def solution(mesh):
    return jax.shard_map(
        per_device,
        mesh=mesh,
        in_specs=(P("tm", None, "space", None, None), P(None, "space", "tm", None)),
        out_specs=P("tm", None, "space", None, None),
        check_vma=False,
    )
```

profile of v0, /device:TPU:104, one launch (start us, length us, event | category | flops | bytes accessed | tf_op | source)
XLA Modules:
  0.0 130.5 jit_solution(3187420438040695835)
XLA Ops:
  0.0 2.2 %copy.686 = f32[4,6,2,32,128]{4,3,2,0,1:T(8,128)} copy(f32[4,6,2,32,128]{4,3,2,1,0:T(8,128)} %param.3) | data formatting | bytes 1572864 | tf_op args[0]
  2.2 1.7 %collective-permute-start.1 = (f32[4,6,2,32,128]{4,3,2,0,1:T(8,128)}, f32[4,6,2,32,128]{4,3,2,0,1:T(8,128)}, u32[]{:S(2)}, u32[]{:S(2)}) collective-permute-start(f32[4,6,2,32,128]{4,3,2,0,1:T(8,128)} %copy.686), channel_id=1, source_target_pairs={{1,0},{2,1},{3,2},{4,3},{5,4},{6,5},{7,6},{8,7},{9,8},{10,9},{11,1... | collective-permute-start | bytes 2359304 | tf_op jit(solution)/shard_map/ppermute | solution.py:32
  3.9 1.5 %copy.725 = f32[4,6,2,32,128]{4,1,2,0,3:T(8,128)} copy(f32[4,6,2,32,128]{4,3,2,1,0:T(8,128)S(1)} %copy-done) | data formatting | bytes 1572864 | tf_op args[0]
  5.5 4.4 %all-to-all-start = ((f32[4,6,2,32,128]{4,1,2,0,3:T(8,128)}), f32[4,6,2,32,128]{4,1,2,0,3:T(8,128)}, u32[]{:S(2)}, u32[]{:S(2)}) async-start(f32[4,6,2,32,128]{4,1,2,0,3:T(8,128)} %copy.725), calls=%async_computation | async-start | bytes 2097152 | tf_op jit(solution)/shard_map/all_to_all | solution.py:158
  9.9 22.6 %all_gather.3 = f32[11,2,32,128]{3,2,1,0:T(8,128)S(1)} all-gather(f32[11,2,8,128]{3,2,1,0:T(8,128)S(1)} %copy-done.47), channel_id=1, replica_groups=mesh['tm'=4,'space'=64] {'tm'}, dimensions={2}, use_global_device_ids=true | all-gather | bytes 450560 | tf_op jit(solution)/shard_map/all_gather | solution.py:128
  32.7 1.7 %collective-permute-start.3 = (f32[11,1,32,128]{3,2,1,0:T(8,128)S(1)}, f32[11,1,32,128]{3,2,1,0:T(8,128)S(1)}, u32[]{:S(2)}, u32[]{:S(2)}) collective-permute-start(f32[11,1,32,128]{3,2,1,0:T(8,128)S(1)} %get-tuple-element.174), channel_id=1, source_target_pairs={{1,0},{2,1},{3,2},{4,3},{5,4},{6,5},{7,6},{8,7},{9,8},{10,9},{11,1... | collective-permute-start | bytes 540680 | tf_op jit(solution)/shard_map/ppermute | solution.py:32
  35.2 1.5 %slice.644 = f32[4,6,2,32,126]{4,3,2,0,1:T(8,128)S(1)} slice(f32[4,6,2,32,128]{4,3,2,0,1:T(8,128)} %copy.686), slice={[0:4], [0:6], [0:2], [0:32], [2:128]} | slice | bytes 1548288 | tf_op jit(solution)/shard_map/jit(_roll_static)/slice | solution.py:185
  37.4 0.9 slice.635
  38.4 1.2 slice.634
  43.4 0.8 fusion.21
  45.1 2.2 %fusion.29 = f32[4,6,2,32,128]{4,3,2,0,1:T(8,128)S(1)} fusion(f32[4,1,2,32,128]{4,3,2,0,1:T(8,128)S(1)} %get-tuple-element.137, f32[4,1,2,32,128]{4,3,2,0,1:T(8,128)S(1)} %get-tuple-element.135, f32[4,3,2,32,128]{4,3,2,0,1:T(8,128)S(1)} %get-tuple-element.140, f32[4,1,2,32,128]{4,3,2,0,1:T(8,128)S(1)} %get-tuple-element.136, ...), kind=kLoop, calls=%fused_computation.57 | loop fusion | flops 5308416 | bytes 6422552 | tf_op jit(solution)/shard_map/sub | solution.py:110
  47.3 1.2 slice.650
  49.9 1.7 %copy.877 = f32[4,6,2,4,8,128]{5,4,2,1,0,3:T(8,128)S(1)} copy(f32[4,6,2,4,8,128]{5,1,2,0,4,3:T(8,128)} %bitcast.62) | data formatting | bytes 1572864 | tf_op jit(solution)/shard_map/all_to_all | solution.py:158
  52.4 1.1 fusion.52
  53.6 1.1 copy.728
  54.7 4.4 %all-to-all-start.1 = ((f32[16,6,2,8,128]{4,3,2,1,0:T(8,128)}), f32[16,6,2,8,128]{4,3,2,1,0:T(8,128)}, u32[]{:S(2)}, u32[]{:S(2)}) async-start(f32[16,6,2,8,128]{4,3,2,1,0:T(8,128)} %copy.728), calls=%async_computation.1 | async-start | bytes 1572864 | tf_op jit(solution)/shard_map/all_to_all | solution.py:163
  59.1 1.2 constant_dynamic-update-slice_fusion.1
  60.5 1.2 constant_dynamic-update-slice_fusion.2
  63.5 1.1 fusion.9
  65.6 0.8 broadcast_multiply_fusion
  66.4 1.4 %fusion.163 = (f32[4,6,2,32,128]{4,3,2,0,1:T(8,128)}, f32[4,6,2,32,128]{4,3,2,0,1:T(8,128)}) fusion(f32[4,6,3,32,128]{4,3,2,0,1:T(8,128)S(1)} %fusion.9), kind=kLoop, calls=%fused_computation.411 | loop fusion | bytes 3145728 | tf_op jit(solution)/shard_map/slice | solution.py:176
  67.8 3.7 %all-to-all-done.1 = f32[16,6,2,8,128]{4,3,2,1,0:T(8,128)} async-done(((f32[16,6,2,8,128]{4,3,2,1,0:T(8,128)}), f32[16,6,2,8,128]{4,3,2,1,0:T(8,128)}, u32[]{:S(2)}, u32[]{:S(2)}) %all-to-all-start.1) | async-done | bytes 786464 | tf_op jit(solution)/shard_map/all_to_all | solution.py:163
  71.5 2.7 %fusion.51 = f32[4,6,2,32,128]{4,3,2,1,0:T(8,128)S(1)} fusion(f32[4,6,2,32,128]{4,3,2,1,0:T(8,128)S(1)} %copy-done, f32[4,4,6,2,8,128]{5,4,3,2,1,0:T(8,128)} %bitcast.65, f32[4,6,2,32,128]{4,3,2,0,1:T(8,128)S(1)} %fusion.29, f32[4,6,2,32,128]{4,3,2,0,1:T(8,128)S(1)} %copy-done.6, f32[4,6,2,32,128]{4,3,2,0,1:T(8,128)} %get-tuple-element.120, ...), kind=kLoop, calls=%fused_computation.90 | loop fusion | flops 2359296 | bytes 7372800 | tf_op jit(solution)/shard_map/sub | solution.py:193
  74.2 1.2 slice.698
  76.0 1.3 fusion.165
  79.0 1.0 slice.680
  80.0 1.7 %collective-permute-start.5 = (f32[4,6,2,32,128]{4,3,2,0,1:T(8,128)S(1)}, f32[4,6,2,32,128]{4,3,2,0,1:T(8,128)}, u32[]{:S(2)}, u32[]{:S(2)}) collective-permute-start(f32[4,6,2,32,128]{4,3,2,0,1:T(8,128)S(1)} %copy.730), channel_id=1, source_target_pairs={{1,0},{2,1},{3,2},{4,3},{5,4},{6,5},{7,6},{8,7},{9,8},{10,9},{11,1... | collective-permute-start | bytes 2359304 | tf_op jit(solution)/shard_map/ppermute | solution.py:32
  81.8 1.5 %copy.777 = f32[4,6,2,32,128]{4,1,2,0,3:T(8,128)} copy(f32[4,6,2,32,128]{4,3,2,1,0:T(8,128)S(1)} %fusion.51) | data formatting | bytes 1572864 | tf_op jit(solution)/shard_map/sub | solution.py:193
  83.3 4.6 %all-to-all-start.2 = ((f32[4,6,2,32,128]{4,1,2,0,3:T(8,128)}), f32[4,6,2,32,128]{4,1,2,0,3:T(8,128)}, u32[]{:S(2)}, u32[]{:S(2)}) async-start(f32[4,6,2,32,128]{4,1,2,0,3:T(8,128)} %copy.777), calls=%async_computation.2 | async-start | bytes 2097152 | tf_op jit(solution)/shard_map/all_to_all | solution.py:158
  87.9 1.8 %fusion.98 = (f32[4,1,2,32,128]{4,3,2,0,1:T(8,128)S(1)}, f32[4,1,2,32,128]{4,3,2,0,1:T(8,128)S(1)}, f32[4,2,32,128]{3,2,1,0:T(8,128)S(1)}, f32[4,1,2,32,128]{4,3,2,1,0:T(8,128)}) fusion(f32[4,6,2,32,128]{4,3,2,1,0:T(8,128)S(1)} %fusion.51, f32[4,6,2,1,128]{4,3,2,0,1:T(1,128)S(1)} %get-tuple-element.147, f32[4,6,2,31,128]{4,3,2,0,1:T(8,128)} %get-tuple-element.149, ...), kind=kLoop, calls=%fused_computation.273 | loop fusion | flops 491520 | bytes 1671168 | tf_op jit(solution)/shard_map/mul | solution.py:100
  89.9 0.9 copy-done.1
  92.3 0.8 bitcast_multiply_fusion.25
  93.2 0.9 fusion.143
  94.1 1.2 multiply_add_fusion.7
  95.3 1.1 maximum_multiply_fusion.4
  98.6 1.2 slice.700
  99.8 4.4 %all-to-all-done.2 = f32[4,6,2,32,128]{4,1,2,0,3:T(8,128)} async-done(((f32[4,6,2,32,128]{4,1,2,0,3:T(8,128)}), f32[4,6,2,32,128]{4,1,2,0,3:T(8,128)}, u32[]{:S(2)}, u32[]{:S(2)}) %all-to-all-start.2) | async-done | bytes 786464 | tf_op jit(solution)/shard_map/all_to_all | solution.py:158
  104.2 2.6 %copy.876 = f32[4,6,2,4,8,128]{5,4,2,1,0,3:T(8,128)} copy(f32[4,6,2,4,8,128]{5,1,2,0,4,3:T(8,128)} %bitcast.110) | data formatting | bytes 1572864 | tf_op jit(solution)/shard_map/all_to_all | solution.py:158
  106.8 1.3 reshape.346
  108.1 0.8 convolution_bitcast_fusion
  108.9 1.0 copy.786
  109.9 4.3 %all-to-all-start.3 = ((f32[16,6,2,8,128]{4,3,2,1,0:T(8,128)}), f32[16,6,2,8,128]{4,3,2,1,0:T(8,128)}, u32[]{:S(2)}, u32[]{:S(2)}) async-start(f32[16,6,2,8,128]{4,3,2,1,0:T(8,128)} %bitcast.136), calls=%async_computation.3 | async-start | bytes 1572864 | tf_op jit(solution)/shard_map/all_to_all | solution.py:163
  114.3 1.3 %constant_dynamic-update-slice_fusion.7 = f32[4,6,4,32,128]{4,3,2,0,1:T(8,128)S(1)} fusion(f32[4,6,2,32,128]{4,3,2,0,1:T(8,128)} %collective-permute-done.4), kind=kLoop, calls=%fused_computation.397 | loop fusion | bytes 1572864
  115.9 2.1 %constant_dynamic-update-slice_fusion.6 = (f32[4,6,4,32,128]{4,3,2,0,1:T(8,128)S(1)}, f32[4,6,4,32,128]{4,3,2,0,1:T(8,128)S(1)}, f32[4,6,2,32,128]{4,3,2,0,1:T(8,128)S(1)}) fusion(f32[4,6,4,32,128]{4,3,2,0,1:T(8,128)S(1)} %constant_dynamic-update-slice_fusion.7, f32[4,6,2,32,128]{4,3,2,1,0:T(8,128)S(1)} %fusion.51, ...), kind=kLoop, calls=%fused_computation.396 | loop fusion | flops 4325375 | bytes 7282688 | tf_op jit(solution)/shard_map/concatenate | solution.py:33
  118.0 1.3 constant_dynamic-update-slice_fusion.8
  122.6 1.9 %copy_subtract_fusion = f32[4,6,3,32,128]{4,3,2,1,0:T(8,128)} fusion(f32[4,6,4,32,128]{4,3,2,0,1:T(8,128)S(1)} %get-tuple-element.143, f32[4,6,4,32,128]{4,3,2,0,1:T(8,128)S(1)} %constant_dynamic-update-slice_fusion.8, f32[4,1,3,32,128]{4,3,2,0,1:T(8,128)S(1)} %get-tuple-element.105, f32[4,1,3,32,128]{4,3,2,0,1:T(8,128)S(1)} %get-tuple-element.103, ...), kind=kLoop, calls=%fused_computation.33 | loop fusion | flops 7077888 | bytes 9634304 | tf_op jit(solution)/shard_map/sub | solution.py:110
  124.5 2.6 %all-to-all-done.3 = f32[16,6,2,8,128]{4,3,2,1,0:T(8,128)} async-done(((f32[16,6,2,8,128]{4,3,2,1,0:T(8,128)}), f32[16,6,2,8,128]{4,3,2,1,0:T(8,128)}, u32[]{:S(2)}, u32[]{:S(2)}) %all-to-all-start.3) | async-done | bytes 786464 | tf_op jit(solution)/shard_map/all_to_all | solution.py:163
  127.1 3.3 %subtract_subtract_fusion = f32[4,6,2,32,128]{4,3,2,1,0:T(8,128)} fusion(f32[4,6,2,32,128]{4,3,2,1,0:T(8,128)S(1)} %copy-done, f32[4,6,2,32,128]{4,3,2,1,0:T(8,128)S(1)} %copy-done.4, f32[4,6,2,32,128]{4,3,2,1,0:T(8,128)S(1)} %copy_subtract_fusion.1, f32[4,6,3,32,128]{4,3,2,1,0:T(8,128)} %copy_subtract_fusion, f32[4,6,2,31,128]{4,3,2,1,0:T(8,128)S(1)} %bitcast.477, ...), kind=kLoop, calls=%fused_computation.11 | loop fusion | flops 2555904 | bytes 7372800 | tf_op jit(solution)/shard_map/sub | solution.py:194
  (174 shorter events, 21.0 us)
Async XLA Ops:
  0.0 3.9 %copy-start = (f32[4,6,2,32,128]{4,3,2,1,0:T(8,128)S(1)}, f32[4,6,2,32,128]{4,3,2,1,0:T(8,128)}, u32[]{:S(2)}) copy-start(f32[4,6,2,32,128]{4,3,2,1,0:T(8,128)} %param.3) | copy-start | bytes 2359300
  2.2 56.9 %collective-permute-start = (f32[4,6,2,32,128]{4,3,2,0,1:T(8,128)}, f32[4,6,2,32,128]{4,3,2,0,1:T(8,128)}, u32[]{:S(2)}, u32[]{:S(2)}) collective-permute-start(f32[4,6,2,32,128]{4,3,2,0,1:T(8,128)} %copy.686), channel_id=1, source_target_pairs={{0,1},{1,2},{2,3},{3,4},{4,5},{5,6},{6,7},{7,8},{8,9},{9,10},{10,1... | collective-permute-start | bytes 2359304 | tf_op jit(solution)/shard_map/ppermute | solution.py:31
  2.2 58.3 %collective-permute-start.1 = (f32[4,6,2,32,128]{4,3,2,0,1:T(8,128)}, f32[4,6,2,32,128]{4,3,2,0,1:T(8,128)}, u32[]{:S(2)}, u32[]{:S(2)}) collective-permute-start(f32[4,6,2,32,128]{4,3,2,0,1:T(8,128)} %copy.686), channel_id=1, source_target_pairs={{1,0},{2,1},{3,2},{4,3},{5,4},{6,5},{7,6},{8,7},{9,8},{10,9},{11,1... | collective-permute-start | bytes 2359304 | tf_op jit(solution)/shard_map/ppermute | solution.py:32
  5.5 4.4 %copy-start.47 = (f32[11,2,8,128]{3,2,1,0:T(8,128)S(1)}, f32[11,2,8,128]{3,2,1,0:T(8,128)}, u32[]{:S(2)}) copy-start(f32[11,2,8,128]{3,2,1,0:T(8,128)} %param.4) | copy-start | bytes 270340
  5.5 44.4 %all-to-all-start = ((f32[4,6,2,32,128]{4,1,2,0,3:T(8,128)}), f32[4,6,2,32,128]{4,1,2,0,3:T(8,128)}, u32[]{:S(2)}, u32[]{:S(2)}) async-start(f32[4,6,2,32,128]{4,1,2,0,3:T(8,128)} %copy.725), calls=%async_computation | async-start | bytes 2097152 | tf_op jit(solution)/shard_map/all_to_all | solution.py:158
  32.6 15.9 %collective-permute-start.2 = (f32[11,1,32,128]{3,2,1,0:T(8,128)S(1)}, f32[11,1,32,128]{3,2,1,0:T(8,128)S(1)}, u32[]{:S(2)}, u32[]{:S(2)}) collective-permute-start(f32[11,1,32,128]{3,2,1,0:T(8,128)S(1)} %get-tuple-element.175), channel_id=1, source_target_pairs={{0,1},{1,2},{2,3},{3,4},{4,5},{5,6},{6,7},{7,8},{8,9},{9,10},{10,1... | collective-permute-start | bytes 540680 | tf_op jit(solution)/shard_map/ppermute | solution.py:31
  32.7 16.6 %collective-permute-start.3 = (f32[11,1,32,128]{3,2,1,0:T(8,128)S(1)}, f32[11,1,32,128]{3,2,1,0:T(8,128)S(1)}, u32[]{:S(2)}, u32[]{:S(2)}) collective-permute-start(f32[11,1,32,128]{3,2,1,0:T(8,128)S(1)} %get-tuple-element.174), channel_id=1, source_target_pairs={{1,0},{2,1},{3,2},{4,3},{5,4},{6,5},{7,6},{8,7},{9,8},{10,9},{11,1... | collective-permute-start | bytes 540680 | tf_op jit(solution)/shard_map/ppermute | solution.py:32
  35.2 7.0 %copy-start.13 = (f32[3,2,32,128]{3,2,1,0:T(8,128)}, f32[3,2,32,128]{3,2,1,0:T(8,128)S(1)}, u32[]{:S(2)}) copy-start(f32[3,2,32,128]{3,2,1,0:T(8,128)S(1)} %get-tuple-element.178) | copy-start | bytes 294916
  35.2 7.0 %copy-start.15 = (f32[3,2,32,128]{3,2,1,0:T(8,128)}, f32[3,2,32,128]{3,2,1,0:T(8,128)S(1)}, u32[]{:S(2)}) copy-start(f32[3,2,32,128]{3,2,1,0:T(8,128)S(1)} %get-tuple-element.179) | copy-start | bytes 294916
  37.3 5.4 %copy-start.38 = (f32[2,32,128]{2,1,0:T(8,128)}, f32[2,32,128]{2,1,0:T(8,128)S(1)}, u32[]{:S(2)}) copy-start(f32[2,32,128]{2,1,0:T(8,128)S(1)} %get-tuple-element.171) | copy-start | bytes 98308
  37.3 5.4 %copy-start.40 = (f32[2,32,128]{2,1,0:T(8,128)}, f32[2,32,128]{2,1,0:T(8,128)S(1)}, u32[]{:S(2)}) copy-start(f32[2,32,128]{2,1,0:T(8,128)S(1)} %get-tuple-element.173) | copy-start | bytes 98308
  40.8 1.0 copy-start.17
  40.8 1.0 copy-start.21
  41.0 2.5 %copy-start.23 = (f32[4,2,32,128]{3,2,1,0:T(8,128)}, f32[4,2,32,128]{3,2,1,0:T(8,128)S(1)}, u32[]{:S(2)}) copy-start(f32[4,2,32,128]{3,2,1,0:T(8,128)S(1)} %get-tuple-element.77) | copy-start | bytes 393220
  42.2 3.0 %copy-start.25 = (f32[4,2,32,128]{3,2,1,0:T(8,128)}, f32[4,2,32,128]{3,2,1,0:T(8,128)S(1)}, u32[]{:S(2)}) copy-start(f32[4,2,32,128]{3,2,1,0:T(8,128)S(1)} %get-tuple-element.117) | copy-start | bytes 393220
  48.6 14.5 %copy-start.7 = (f32[3,3,32,128]{3,2,1,0:T(8,128)}, f32[3,3,32,128]{3,2,1,0:T(8,128)S(1)}, u32[]{:S(2)}) copy-start(f32[3,3,32,128]{3,2,1,0:T(8,128)S(1)} %get-tuple-element.169) | copy-start | bytes 442372
  54.7 16.8 %all-to-all-start.1 = ((f32[16,6,2,8,128]{4,3,2,1,0:T(8,128)}), f32[16,6,2,8,128]{4,3,2,1,0:T(8,128)}, u32[]{:S(2)}, u32[]{:S(2)}) async-start(f32[16,6,2,8,128]{4,3,2,1,0:T(8,128)} %copy.728), calls=%async_computation.1 | async-start | bytes 1572864 | tf_op jit(solution)/shard_map/all_to_all | solution.py:163
  64.5 1.0 copy-start.22
  64.6 1.0 copy-start.32
  64.6 1.0 copy-start.45
  66.4 5.1 %copy-start.6 = (f32[4,6,2,32,128]{4,3,2,0,1:T(8,128)S(1)}, f32[4,6,2,32,128]{4,3,2,0,1:T(8,128)}, u32[]{:S(2)}) copy-start(f32[4,6,2,32,128]{4,3,2,0,1:T(8,128)} %copy-done.5) | copy-start | bytes 2359300
  66.4 5.1 %copy-start.29 = (f32[4,1,2,32,128]{4,3,2,1,0:T(8,128)S(1)}, f32[4,1,2,32,128]{4,3,2,1,0:T(8,128)}, u32[]{:S(2)}) copy-start(f32[4,1,2,32,128]{4,3,2,1,0:T(8,128)} %get-tuple-element.152) | copy-start | bytes 393220
  66.4 5.1 %copy-start.31 = (f32[4,2,32,128]{3,2,1,0:T(8,128)S(1)}, f32[4,2,32,128]{3,2,1,0:T(8,128)}, u32[]{:S(2)}) copy-start(f32[4,2,32,128]{3,2,1,0:T(8,128)} %get-tuple-element.68) | copy-start | bytes 393220
  66.4 5.1 %copy-start.46 = (f32[4,6,2,1,128]{4,3,2,0,1:T(1,128)S(1)}, f32[4,6,2,1,128]{4,3,2,0,1:T(1,128)}, u32[]{:S(2)}) copy-start(f32[4,6,2,1,128]{4,3,2,0,1:T(1,128)} %slice.640) | copy-start | bytes 73732
  78.3 36.0 %collective-permute-start.4 = (f32[4,6,2,32,128]{4,3,2,0,1:T(8,128)S(1)}, f32[4,6,2,32,128]{4,3,2,0,1:T(8,128)}, u32[]{:S(2)}, u32[]{:S(2)}) collective-permute-start(f32[4,6,2,32,128]{4,3,2,0,1:T(8,128)S(1)} %copy.730), channel_id=1, source_target_pairs={{0,1},{1,2},{2,3},{3,4},{4,5},{5,6},{6,7},{7,8},{8,9},{9,10},{10,1... | collective-permute-start | bytes 2359304 | tf_op jit(solution)/shard_map/ppermute | solution.py:31
  80.0 37.9 %collective-permute-start.5 = (f32[4,6,2,32,128]{4,3,2,0,1:T(8,128)S(1)}, f32[4,6,2,32,128]{4,3,2,0,1:T(8,128)}, u32[]{:S(2)}, u32[]{:S(2)}) collective-permute-start(f32[4,6,2,32,128]{4,3,2,0,1:T(8,128)S(1)} %copy.730), channel_id=1, source_target_pairs={{1,0},{2,1},{3,2},{4,3},{5,4},{6,5},{7,6},{8,7},{9,8},{10,9},{11,1... | collective-permute-start | bytes 2359304 | tf_op jit(solution)/shard_map/ppermute | solution.py:32
  83.3 4.6 %copy-start.39 = (f32[2,32,128]{2,1,0:T(8,128)S(1)}, f32[2,32,128]{2,1,0:T(8,128)}, u32[]{:S(2)}) copy-start(f32[2,32,128]{2,1,0:T(8,128)} %copy-done.38) | copy-start | bytes 98308
  83.3 4.6 %copy-start.41 = (f32[2,32,128]{2,1,0:T(8,128)S(1)}, f32[2,32,128]{2,1,0:T(8,128)}, u32[]{:S(2)}) copy-start(f32[2,32,128]{2,1,0:T(8,128)} %copy-done.40) | copy-start | bytes 98308
  83.3 4.6 %copy-start.43 = (f32[2,32,128]{2,1,0:T(8,128)S(1)}, f32[2,32,128]{2,1,0:T(8,128)}, u32[]{:S(2)}) copy-start(f32[2,32,128]{2,1,0:T(8,128)} %copy-done.42) | copy-start | bytes 98308
  83.3 20.9 %all-to-all-start.2 = ((f32[4,6,2,32,128]{4,1,2,0,3:T(8,128)}), f32[4,6,2,32,128]{4,1,2,0,3:T(8,128)}, u32[]{:S(2)}, u32[]{:S(2)}) async-start(f32[4,6,2,32,128]{4,1,2,0,3:T(8,128)} %copy.777), calls=%async_computation.2 | async-start | bytes 2097152 | tf_op jit(solution)/shard_map/all_to_all | solution.py:158
  87.9 1.8 %copy-start.37 = (f32[2,32,128]{2,1,0:T(8,128)S(1)}, f32[2,32,128]{2,1,0:T(8,128)}, u32[]{:S(2)}) copy-start(f32[2,32,128]{2,1,0:T(8,128)} %copy-done.36) | copy-start | bytes 98308
  89.7 1.1 copy-start.1
  89.7 1.1 copy-start.27
  90.9 0.9 copy-start.16
  96.7 1.1 copy-start.11
  96.8 1.1 copy-start.26
  98.6 8.2 %copy-start.3 = (f32[4,6,2,32,128]{4,3,2,1,0:T(8,128)}, f32[4,6,2,32,128]{4,3,2,1,0:T(8,128)S(1)}, u32[]{:S(2)}) copy-start(f32[4,6,2,32,128]{4,3,2,1,0:T(8,128)S(1)} %fusion.48) | copy-start | bytes 2359300
  106.8 1.3 copy-start.48
  109.9 5.7 %copy-start.24 = (f32[4,2,32,128]{3,2,1,0:T(8,128)S(1)}, f32[4,2,32,128]{3,2,1,0:T(8,128)}, u32[]{:S(2)}) copy-start(f32[4,2,32,128]{3,2,1,0:T(8,128)} %copy-done.23) | copy-start | bytes 393220
  109.9 5.7 %copy-start.30 = (f32[4,1,2,32,128]{4,3,2,0,1:T(8,128)S(1)}, f32[4,1,2,32,128]{4,3,2,0,1:T(8,128)}, u32[]{:S(2)}) copy-start(f32[4,1,2,32,128]{4,3,2,0,1:T(8,128)} %get-tuple-element.123) | copy-start | bytes 393220
  109.9 5.7 %copy-start.44 = (f32[4,6,2,2,128]{4,3,2,0,1:T(2,128)S(1)}, f32[4,6,2,2,128]{4,3,2,0,1:T(2,128)}, u32[]{:S(2)}) copy-start(f32[4,6,2,2,128]{4,3,2,0,1:T(2,128)} %slice.681) | copy-start | bytes 147460
  109.9 17.2 %all-to-all-start.3 = ((f32[16,6,2,8,128]{4,3,2,1,0:T(8,128)}), f32[16,6,2,8,128]{4,3,2,1,0:T(8,128)}, u32[]{:S(2)}, u32[]{:S(2)}) async-start(f32[16,6,2,8,128]{4,3,2,1,0:T(8,128)} %bitcast.136), calls=%async_computation.3 | async-start | bytes 1572864 | tf_op jit(solution)/shard_map/all_to_all | solution.py:163
  114.3 1.4 %copy-start.2 = (f32[4,6,2,31,128]{4,3,2,0,1:T(8,128)S(1)}, f32[4,6,2,31,128]{4,3,2,0,1:T(8,128)}, u32[]{:S(2)}) copy-start(f32[4,6,2,31,128]{4,3,2,0,1:T(8,128)} %get-tuple-element.149) | copy-start | bytes 2285572
  114.3 1.6 %copy-start.9 = (f32[4,6,2,30,128]{4,3,2,0,1:T(8,128)S(1)}, f32[4,6,2,30,128]{4,3,2,0,1:T(8,128)}, u32[]{:S(2)}) copy-start(f32[4,6,2,30,128]{4,3,2,0,1:T(8,128)} %slice.680) | copy-start | bytes 2211844
  118.0 1.4 %copy-start.12 = (f32[4,6,2,32,128]{4,3,2,0,1:T(8,128)S(1)}, f32[4,6,2,32,128]{4,3,2,0,1:T(8,128)}, u32[]{:S(2)}) copy-start(f32[4,6,2,32,128]{4,3,2,0,1:T(8,128)} %get-tuple-element.203) | copy-start | bytes 2359300
  122.6 4.5 %copy-start.4 = (f32[4,6,2,32,128]{4,3,2,1,0:T(8,128)S(1)}, f32[4,6,2,32,128]{4,3,2,1,0:T(8,128)}, u32[]{:S(2)}) copy-start(f32[4,6,2,32,128]{4,3,2,1,0:T(8,128)} %copy-done.3) | copy-start | bytes 2359300
  122.6 4.5 %copy-start.10 = (f32[4,6,2,32,1]{4,3,2,1,0:T(8,128)S(1)}, f32[4,6,2,32,1]{4,3,2,1,0:T(8,128)}, u32[]{:S(2)}) copy-start(f32[4,6,2,32,1]{4,3,2,1,0:T(8,128)} %slice.700) | copy-start | bytes 18436
  122.6 4.5 %copy-start.28 = (f32[4,2,32,128]{3,2,1,0:T(8,128)S(1)}, f32[4,2,32,128]{3,2,1,0:T(8,128)}, u32[]{:S(2)}) copy-start(f32[4,2,32,128]{3,2,1,0:T(8,128)} %get-tuple-element.69) | copy-start | bytes 393220
  (12 other events, 9.9 us)
where the time goes:
time: 132 us; the launch traced here: 130 us
  local copies, waits for them, and re-layouts  40.9 us (31%)
  other arithmetic  30.3 us (23%)
  starting transfers between devices  23.1 us (18%)
  blocking collectives  22.6 us (17%)
  waiting for transfers between devices  10.8 us (8%)
  matrix products  1.93 us (1%)
    all_gather x1, blocking collectives, per_device(): assembled = lax.all_gather(metrics, 'tm', axis=2, tiled=True)  22.6 us
    unnamed x108, local copies, waits for them, and re-layouts  14.2 us
    all_to_all x2, starting transfers between devices, per_device(): lax.all_to_all(current, 'tm', split_axis=3, concat_axis=0, tiled=True)  9.01 us
    all_to_all x2, starting transfers between devices, per_device(): lax.all_to_all(mixed, 'tm', split_axis=0, concat_axis=3, tiled=True)  8.69 us
    sub x6, other arithmetic, face_flux(): return central - damping - conduct[:, None] * viscous  6.75 us
    all_to_all x2, waiting for transfers between devices, per_device(): lax.all_to_all(mixed, 'tm', split_axis=0, concat_axis=3, tiled=True)  6.33 us
    slice x6, local copies, waits for them, and re-layouts, per_device(): jnp.roll(current, -2, axis_state)  5.58 us
    ppermute x3, starting transfers between devices, with_halo(): after = lax.ppermute(leading, axis, down)  5.21 us
  transfers between devices with their start and end apart: 10, of which 3 were waited for; matrix products, arithmetic and copies ran while one was open for 41% of the time, Pallas kernels for 0%

commit v1 on v0

v1 whole, which is shorter than its diff:
```python
import math

import jax
import jax.numpy as jnp
from jax import lax
from jax.experimental import pallas as pl
from jax.experimental.pallas import tpu as pltpu
from jax.sharding import PartitionSpec as P

NINST = 16
GROUPS = 4
PER = 4
TILES = 12
GAMMA = 1.4
EPS_TWO = 0.1
EPS_FOUR = 0.03125
JUMP_RATIO = (EPS_TWO + 3.0 * EPS_FOUR) / EPS_FOUR
VISCOSITY = 0.02
HEAT_FACTOR = 1.4 / (0.4 * 0.72)
TURB_DIFFUSE = 1.5
WALL_COEFF = 3.24
MESH = pl.DeviceIdType.MESH


def table_entry(offset):
    offset = offset % NINST
    if offset == 0 or offset == NINST // 2:
        return 0.0
    parity = 1.0 if offset % 2 == 0 else -1.0
    return 0.5 * parity / math.tan(math.pi * offset / NINST)


def lane_roll(x, k):
    k = k % 128
    return x if k == 0 else pltpu.roll(x, k, 1)


def row_roll(x, k):
    k = k % 8
    return x if k == 0 else pltpu.roll(x, k, 0)


class Masks:
    def __init__(self):
        lane = lax.broadcasted_iota(jnp.int32, (8, 128), 1)
        self.row = lax.broadcasted_iota(jnp.int32, (8, 128), 0)
        self.zlo = lane & 31
        self.half = lane < 64
        self.even = (lane & 32) == 0


def swap_segments(m, x):
    a0 = jnp.where(m.half, x[0], lane_roll(x[2], 64))
    a2 = jnp.where(m.half, lane_roll(x[0], 64), x[2])
    a1 = jnp.where(m.half, x[1], lane_roll(x[3], 64))
    a3 = jnp.where(m.half, lane_roll(x[1], 64), x[3])
    return [
        jnp.where(m.even, a0, lane_roll(a1, 32)),
        jnp.where(m.even, lane_roll(a0, -32), a1),
        jnp.where(m.even, a2, lane_roll(a3, 32)),
        jnp.where(m.even, lane_roll(a2, -32), a3),
    ]


def pack_edge(m, acc, tile, k, first):
    moved = lane_roll(tile, 2 * k - first)
    return moved if acc is None else jnp.where((m.zlo >> 1) == k, moved, acc)


def y_up(m, w, w32, k):
    return row_roll(jnp.where(m.row < k, w32, w), -k)


def y_down(m, w, k):
    return row_roll(jnp.where(m.row >= 8 - k, lane_roll(w, 32), w), k)


def primitives(w):
    inv = 1.0 / w[0]
    u = [w[1] * inv, w[2] * inv, w[3] * inv]
    kin = 0.5 * (w[1] * u[0] + w[2] * u[1] + w[3] * u[2])
    p = (GAMMA - 1.0) * (w[4] - kin)
    temp = p * inv
    return dict(
        u=u,
        p=p,
        h=w[4] + p,
        e=kin * inv + HEAT_FACTOR * temp,
        n=TURB_DIFFUSE * (w[5] * inv),
        t=temp,
    )


def half_sound(prim):
    return 0.5 * jnp.sqrt(GAMMA * prim["t"])


def dot3(a, b):
    return a[0] * b[0] + a[1] * b[1] + a[2] * b[2]


def face(wm, wl, wr, wp, pl_, pr_, geo, scaled=None):
    hs, length, cond = geo[0:3], geo[3], geo[4]
    ql = dot3(pl_["u"], hs)
    qr = dot3(pr_["u"], hs)
    rad = None
    if scaled is None:
        rad = jnp.abs(ql + qr) + (half_sound(pl_) + half_sound(pr_)) * length
        scaled = EPS_FOUR * rad
    g = (VISCOSITY + 0.5 * (wl[5] + wr[5])) * cond
    psum = pl_["p"] + pr_["p"]
    out = []
    for f in range(6):
        if f == 4:
            c = pl_["h"] * ql + pr_["h"] * qr
        else:
            c = wl[f] * ql + wr[f] * qr
        if 1 <= f <= 3:
            c = c + psum * hs[f - 1] - g * (pr_["u"][f - 1] - pl_["u"][f - 1])
        if f == 4:
            c = c - g * (pr_["e"] - pl_["e"])
        if f == 5:
            c = c - g * (pr_["n"] - pl_["n"])
        d = wr[f] - wl[f]
        out.append(c - scaled * (JUMP_RATIO * d - (wp[f] - wm[f])))
    return out, rad, scaled


def geometry(s, left_volume, right_volume):
    sq = dot3(s, s)
    return [0.5 * s[0], 0.5 * s[1], 0.5 * s[2], jnp.sqrt(sq), sq / (0.5 * (left_volume + right_volume))]


def geometry_known(s, cond):
    return [0.5 * s[0], 0.5 * s[1], 0.5 * s[2], jnp.sqrt(dot3(s, s)), cond]


def kernel(
    flow, metrics, out,
    xv, mv, sbuf, region, hl0, hr0, res, w1, zs, z1, hl1, hr1, ob, oin, ov,
    ms, mr, mt, mleft, mright, gx, gy, gz, ry, rz, rx, den, step,
    in_sem, own_sem, out_sem, met_s, met_r, pm_s, pm_r,
    xin_s, xin_r, fw_s, fw_r, wp_s, wp_r, z_s, z_r, o_s, o_r,
):
    t = lax.axis_index("tm")
    s = lax.axis_index("space")
    nt = lax.axis_size("tm")
    ns = lax.axis_size("space")
    right = (t, lax.rem(s + 1, ns))
    left = (t, lax.rem(s + ns - 1, ns))

    def group(k):
        return lax.rem(t + k, nt)

    def remote(src, dst, ss, rs, dev):
        return pltpu.make_async_remote_copy(
            src_ref=src, dst_ref=dst, send_sem=ss, recv_sem=rs, device_id=dev, device_id_type=MESH
        )

    barrier = pltpu.get_barrier_semaphore()
    for dev in ((group(1), s), (group(2), s), (group(3), s), left, right):
        pl.semaphore_signal(barrier, inc=1, device_id=dev, device_id_type=MESH)

    load_m = pltpu.make_async_copy(metrics, mv, in_sem.at[PER])
    load_m.start()

    def load_x(j):
        return pltpu.make_async_copy(flow.at[j], xv.at[j], in_sem.at[j])

    for j in range(PER):
        load_x(j).start()

    m = Masks()
    load_m.wait()
    for quad in range(8):
        tiles = []
        for e in range(4 * quad, 4 * quad + 4):
            p, e = divmod(e, 16)
            sz = [mv[6 + c, p] for c in range(3)]
            vol = mv[9, p]
            if e < 3:
                tiles.append(mv[e, p])
            elif e == 3:
                tiles.append(vol)
            elif e < 7:
                tiles.append(mv[e - 1, p])
            elif e < 10:
                tiles.append(sz[e - 7])
            elif e < 13:
                tiles.append(lane_roll(sz[e - 10], 1))
            elif e < 15:
                cond = dot3(sz, sz) / (0.5 * (vol + lane_roll(vol, -1)))
                tiles.append(cond if e == 13 else lane_roll(cond, 1))
            else:
                tiles.append(WALL_COEFF * vol / (mv[10, p] * mv[10, p]))
        for b, tile in enumerate(swap_segments(m, tiles)):
            ms[b, quad] = tile

    def pack(j):
        load_x(j).wait()
        low = [None] * 4
        high = [None] * 4
        for q in range(TILES):
            f, p = divmod(q, 2)
            tiles = swap_segments(m, [xv[j, f, p, 8 * y : 8 * y + 8, :] for y in range(4)])
            for b in range(4):
                sbuf[b, j, q] = tiles[b]
                low[b] = pack_edge(m, low[b], tiles[b], q, 0)
                high[b] = pack_edge(m, high[b], tiles[b], q, 30)
        for b in range(4):
            sbuf[(b + 1) % 4, j, TILES] = high[b]
            sbuf[(b + 3) % 4, j, TILES + 1] = low[b]

    def met_copy(k):
        return remote(ms.at[group(k)], mr.at[t], met_s.at[k - 1], met_r.at[k - 1], (group(k), s))

    def met_arrival(k):
        return remote(ms.at[t], mr.at[group(4 - k)], met_s.at[k - 1], met_r.at[k - 1], (group(k), s))

    def xin_copy(k, j):
        return remote(
            sbuf.at[group(k), j], region.at[t * PER + j],
            xin_s.at[k - 1, j], xin_r.at[k - 1, j], (group(k), s),
        )

    def xin_arrival(k, j):
        return remote(
            sbuf.at[t, j], region.at[group(4 - k) * PER + j],
            xin_s.at[k - 1, j], xin_r.at[k - 1, j], (group(k), s),
        )

    def forward(src, i):
        return (
            remote(src, hl0.at[i], fw_s.at[0, i], fw_r.at[0, i], right),
            remote(src, hr0.at[i], fw_s.at[1, i], fw_r.at[1, i], left),
        )

    def own_copy(j):
        return pltpu.make_async_copy(sbuf.at[t, j], region.at[t * PER + j], own_sem.at[j])

    mr[t] = ms[t]
    pl.semaphore_wait(barrier, 5)
    for k in (2, 1, 3):
        met_copy(k).start()

    @pl.loop(0, PER)
    def _(j):
        pack(j)
        for k in (2, 1, 3):
            xin_copy(k, j).start()
        for c in forward(sbuf.at[t, j, pl.ds(0, TILES)], t * PER + j):
            c.start()
        own_copy(j).start()

    for k in (2, 1, 3):
        met_arrival(k).wait_recv()
    for quad in range(8):
        for e, tile in enumerate(swap_segments(m, [mr[b, quad] for b in range(4)])):
            mt[4 * quad + e] = tile
    plane_metrics = (
        remote(mt.at[pl.ds(16, 4)], mleft, pm_s.at[0], pm_r.at[0], right),
        remote(mt.at[pl.ds(3, 1)], mright, pm_s.at[1], pm_r.at[1], left),
    )
    for c in plane_metrics:
        c.start()
    for p in range(2):
        o = 16 * p
        vol = mt[o + 3]
        sy = [mt[o + 4 + c] for c in range(3)]
        geo_y = geometry(sy, vol, y_up(m, vol, lane_roll(vol, -32), 1))
        geo_z = geometry_known([mt[o + 7 + c] for c in range(3)], mt[o + 13])
        geo_l = geometry_known([mt[o + 10 + c] for c in range(3)], mt[o + 14])
        for c in range(5):
            gy[p, c] = geo_y[c]
            gz[p, 0, c] = geo_z[c]
            gz[p, 1, c] = geo_l[c]

    def cross(i, w_of, low_pack, high_pack, first):
        for p in range(2):
            w = [w_of(f, p) for f in range(6)]
            prim = primitives(w)
            yu, yuu, yd, zu, zuu, zd, zdd = [], [], [], [], [], [], []
            for f in range(6):
                k = 2 * f + p
                w32 = lane_roll(w[f], -32)
                yu.append(y_up(m, w[f], w32, 1))
                yuu.append(y_up(m, w[f], w32, 2))
                yd.append(y_down(m, w[f], 1))
                hi = lane_roll(high_pack, 32 - 2 * k)
                lo = lane_roll(low_pack, -2 - 2 * k)
                zu.append(lane_roll(jnp.where(m.zlo == 0, hi, w[f]), -1))
                zuu.append(lane_roll(jnp.where(m.zlo < 2, hi, w[f]), -2))
                zd.append(lane_roll(jnp.where(m.zlo == 31, lo, w[f]), 1))
                zdd.append(lane_roll(jnp.where(m.zlo >= 30, lo, w[f]), 2))
            geo_y = [gy[p, c] for c in range(5)]
            geo_z = [gz[p, 0, c] for c in range(5)]
            geo_l = [gz[p, 1, c] for c in range(5)]
            known = (None, None, None) if first else (ry[i, p], rz[i, p, 0], rz[i, p, 1])
            fy, rad_y, sc_y = face(yd, w, yu, yuu, prim, primitives(yu), geo_y, known[0])
            fz, rad_z, sc_z = face(zd, w, zu, zuu, prim, primitives(zu), geo_z, known[1])
            fl, rad_l, sc_l = face(zdd, zd, w, zu, primitives(zd), prim, geo_l, known[2])
            if first:
                ry[i, p] = sc_y
                rz[i, p, 0] = sc_z
                rz[i, p, 1] = sc_l
                den[i, p] = rad_y + y_down(m, rad_y, 1) + rad_z + rad_l + 8.0 * mt[16 * p + 3]
            for f in range(6):
                r = fy[f] - y_down(m, fy[f], 1) + fz[f] - fl[f]
                if f == 5:
                    r = r + mt[16 * p + 15] * w[5] * w[5] / w[0]
                if not first:
                    r = r + res[i, 2 * f + p]
                res[i, 2 * f + p] = r

    def mix(w_of, first):
        pc = [0.5 * (table_entry(d) + table_entry(d - 8)) for d in range(5)]
        qc = [0.5 * (table_entry(d) - table_entry(d - 8)) for d in range(5)]

        @pl.loop(0, TILES)
        def _(q):
            vol = mt[lax.rem(q, 2) * 16 + 3]
            w = [w_of(i, q) for i in range(NINST)]
            b = [w[i] + w[i + 8] for i in range(8)]
            a = [w[i] - w[i + 8] for i in range(8)]
            a = a + [-x for x in a]
            for r in range(8):
                even = None
                odd = qc[4] * a[(r - 4) % 16]
                for d in range(1, 4):
                    e = pc[d] * (b[(r - d) % 8] - b[(r + d) % 8])
                    even = e if even is None else even + e
                    odd = odd + qc[d] * (a[(r - d) % 16] - a[(r + d) % 16])
                for i, v in ((r, even + odd), (r + 8, even - odd)):
                    v = vol * v
                    res[i, q] = res[i, q] + v if first else v

    def axial(i, w_of, hl, hr, first):
        planes = [
            [hl[i, 2 * f] for f in range(6)],
            [hl[i, 2 * f + 1] for f in range(6)],
            [w_of(f, 0) for f in range(6)],
            [w_of(f, 1) for f in range(6)],
            [hr[i, 2 * f] for f in range(6)],
            [hr[i, 2 * f + 1] for f in range(6)],
        ]
        prims = [primitives(w) for w in planes[1:5]]
        fluxes, radii = [], []
        for k in range(3):
            geo = [gx[k, c] for c in range(5)]
            fx, rad, sc = face(
                planes[k], planes[k + 1], planes[k + 2], planes[k + 3],
                prims[k], prims[k + 1], geo, None if first else rx[i, k],
            )
            if first:
                rx[i, k] = sc
            fluxes.append(fx)
            radii.append(rad)
        result = []
        for p in range(2):
            if first:
                h = 0.5 / (den[i, p] + radii[p] + radii[p + 1])
                step[i, p] = h
            else:
                h = step[i, p]
            result.append([h * (res[i, 2 * f + p] + (fluxes[p + 1][f] - fluxes[p][f])) for f in range(6)])
        return result

    @pl.loop(0, NINST)
    def _(n):
        own = n < PER
        far = jnp.maximum(n - PER, 0)
        j = jnp.where(own, n, far // 3)
        back = jnp.where(own, 0, lax.rem(far, 3) + 1)
        i = lax.rem(t + nt - back, nt) * PER + j

        @pl.when(own)
        def _():
            own_copy(j).wait()

        @pl.when(n >= PER)
        def _():
            xin_arrival(back, j).wait_recv()
            for c in forward(region.at[i, pl.ds(0, TILES)], i):
                c.start()

        cross(i, lambda f, p: region[i, 2 * f + p], region[i, TILES], region[i, TILES + 1], True)

    mix(lambda i, q: region[i, q], True)

    for c in plane_metrics:
        c.wait_recv()
    sx = [[mleft[c] for c in range(3)], [mt[c] for c in range(3)], [mt[16 + c] for c in range(3)]]
    vx = [mleft[3], mt[3], mt[19], mright[0]]
    for k in range(3):
        for c, g in enumerate(geometry(sx[k], vx[k], vx[k + 1])):
            gx[k, c] = g

    def order(n):
        return group(lax.rem(n, 4)) * PER + n // 4

    def edge_copies(i):
        return (
            remote(w1.at[i], hl1.at[i], wp_s.at[0, i], wp_r.at[0, i], right),
            remote(w1.at[i], hr1.at[i], wp_s.at[1, i], wp_r.at[1, i], left),
            remote(zs.at[i, 0], z1.at[i, 1], z_s.at[0, i], z_r.at[0, i], (group(3), s)),
            remote(zs.at[i, 1], z1.at[i, 0], z_s.at[1, i], z_r.at[1, i], (group(1), s)),
        )

    @pl.loop(0, NINST)
    def _(n):
        i = order(n)
        for c in forward(region.at[i, pl.ds(0, TILES)], i):
            c.wait_recv()
        change = axial(i, lambda f, p: region[i, 2 * f + p], hl0, hr0, True)
        low = high = None
        for q in range(TILES):
            f, p = divmod(q, 2)
            v = region[i, q] - 0.5 * change[p][f]
            w1[i, q] = v
            low = pack_edge(m, low, v, q, 0)
            high = pack_edge(m, high, v, q, 30)
        zs[i, 0] = low
        zs[i, 1] = high
        for c in edge_copies(i):
            c.start()

    mix(lambda i, q: w1[i, q], False)

    @pl.loop(0, NINST)
    def _(n):
        i = order(n)
        for c in edge_copies(i)[2:]:
            c.wait_recv()
        cross(i, lambda f, p: w1[i, 2 * f + p], z1[i, 0], z1[i, 1], False)

    def out_copy(k, j):
        g = group(k)
        return remote(
            ob.at[g * PER + j], oin.at[t, j], o_s.at[k - 1, j], o_r.at[k - 1, j], (g, s)
        )

    def out_arrival(k, j):
        return remote(
            ob.at[t * PER + j], oin.at[group(4 - k), j],
            o_s.at[k - 1, j], o_r.at[k - 1, j], (group(k), s),
        )

    def store_out(j):
        return pltpu.make_async_copy(ov.at[j], out.at[j], out_sem.at[j])

    @pl.loop(0, PER)
    def _(j):
        @pl.loop(0, 4)
        def _(k):
            g = group(k)
            i = g * PER + j
            for c in edge_copies(i)[:2]:
                c.wait_recv()
            change = axial(i, lambda f, p: w1[i, 2 * f + p], hl1, hr1, False)
            for q in range(TILES):
                f, p = divmod(q, 2)
                ob[i, q] = -change[p][f]

            @pl.when(k > 0)
            def _():
                out_copy(k, j).start()

            @pl.when(k == 0)
            def _():
                for q in range(TILES):
                    oin[t, j, q] = ob[i, q]

    @pl.loop(0, PER)
    def _(j):
        for k in range(1, 4):
            out_arrival(k, j).wait_recv()
        for q in range(TILES):
            f, p = divmod(q, 2)
            tiles = swap_segments(m, [oin[b, j, q] for b in range(4)])
            for y in range(4):
                ov[j, f, p, 8 * y : 8 * y + 8, :] = tiles[y]
        store_out(j).start()

    for k in (1, 2, 3):
        met_copy(k).wait_send()
    for c in plane_metrics:
        c.wait_send()

    @pl.loop(0, PER)
    def _(j):
        for k in (1, 2, 3):
            xin_copy(k, j).wait_send()
            out_copy(k, j).wait_send()

    @pl.loop(0, NINST)
    def _(i):
        for c in forward(region.at[i, pl.ds(0, TILES)], i):
            c.wait_send()
        for c in edge_copies(i):
            c.wait_send()

    for j in range(PER):
        store_out(j).wait()


def per_device(flow_state, metrics):
    tile = (8, 128)
    f32 = jnp.float32

    def vmem(*lead):
        return pltpu.VMEM(lead + tile, f32)

    dma = pltpu.SemaphoreType.DMA
    full = (NINST, TILES)
    return pl.pallas_call(
        kernel,
        out_shape=jax.ShapeDtypeStruct(flow_state.shape, f32),
        in_specs=[pl.BlockSpec(memory_space=pl.ANY)] * 2,
        out_specs=pl.BlockSpec(memory_space=pl.ANY),
        scratch_shapes=[
            pltpu.VMEM(flow_state.shape, f32),
            pltpu.VMEM(metrics.shape, f32),
            vmem(GROUPS, PER, TILES + 2),
            vmem(NINST, TILES + 2),
            vmem(*full),
            vmem(*full),
            vmem(*full),
            vmem(*full),
            vmem(NINST, 2),
            vmem(NINST, 2),
            vmem(*full),
            vmem(*full),
            vmem(*full),
            vmem(GROUPS, PER, TILES),
            pltpu.VMEM(flow_state.shape, f32),
            vmem(4, 8),
            vmem(4, 8),
            vmem(32),
            vmem(4),
            vmem(1),
            vmem(3, 5),
            vmem(2, 5),
            vmem(2, 2, 5),
            vmem(NINST, 2),
            vmem(NINST, 2, 2),
            vmem(NINST, 3),
            vmem(NINST, 2),
            vmem(NINST, 2),
            dma((PER + 1,)),
            dma((PER,)),
            dma((PER,)),
            dma((3,)),
            dma((3,)),
            dma((2,)),
            dma((2,)),
            dma((3, PER)),
            dma((3, PER)),
            dma((2, NINST)),
            dma((2, NINST)),
            dma((2, NINST)),
            dma((2, NINST)),
            dma((2, NINST)),
            dma((2, NINST)),
            dma((3, PER)),
            dma((3, PER)),
        ],
        compiler_params=pltpu.CompilerParams(
            collective_id=0, has_side_effects=True, vmem_limit_bytes=32 << 20
        ),
        cost_estimate=pl.CostEstimate(
            flops=100_000_000, bytes_accessed=1_800_000, transcendentals=200_000
        ),
        name="balance",
    )(flow_state, metrics)


def solution(mesh):
    return jax.shard_map(
        per_device,
        mesh=mesh,
        in_specs=(P("tm", None, "space", None, None), P(None, "space", "tm", None)),
        out_specs=P("tm", None, "space", None, None),
        check_vma=False,
    )
```

time: 132 us -> 43.4 us (0.33)
  the two profiles are of different devices: /device:TPU:104 before, /device:TPU:2 now
where the time goes in v1:
time: 43.4 us; the launch traced here: 43.1 us
  Pallas kernels  40.2 us (93%)
  local copies, waits for them, and re-layouts  2.9 us (7%)
    pallas_call x1, Pallas kernels, per_device(): pl.pallas_call(kernel, out_shape=jax.ShapeDtypeStruct(flow_state.shape, f...  40.2 us
    unnamed x5, local copies, waits for them, and re-layouts  2.9 us

profile of v1, /device:TPU:2, one launch (start us, length us, event | category | flops | bytes accessed | tf_op | source)
XLA Modules:
  0.0 43.1 jit_solution(17760619530895337544)
XLA Ops:
  0.0 0.0 copy-start
  0.0 1.1 %copy-done = f32[4,6,2,32,128]{4,3,2,1,0:T(8,128)S(1)} copy-done((f32[4,6,2,32,128]{4,3,2,1,0:T(8,128)S(1)}, f32[4,6,2,32,128]{4,3,2,1,0:T(8,128)}, u32[]{:S(2)}) %copy-start) | copy-done | bytes 786456
  1.1 0.0 copy-start.1
  1.1 0.9 %copy-done.1 = f32[11,2,8,128]{3,2,1,0:T(8,128)S(1)} copy-done((f32[11,2,8,128]{3,2,1,0:T(8,128)S(1)}, f32[11,2,8,128]{3,2,1,0:T(8,128)}, u32[]{:S(2)}) %copy-start.1) | copy-done | bytes 90136
  2.0 40.2 %balance.1 = f32[4,6,2,32,128]{4,3,2,1,0:T(8,128)S(1)} custom-call(f32[4,6,2,32,128]{4,3,2,1,0:T(8,128)S(1)} %copy-done, f32[11,2,8,128]{3,2,1,0:T(8,128)S(1)} %copy-done.1), custom_call_target="tpu_custom_call" | custom-call | flops 100000000 | bytes 1800000 | tf_op jit(solution)/shard_map/balance/pallas_call | solution.py:515
  42.3 0.9 %copy.4 = f32[4,6,2,32,128]{4,3,2,1,0:T(8,128)} copy(f32[4,6,2,32,128]{4,3,2,1,0:T(8,128)S(1)} %balance.1) | data formatting | bytes 1572864
Async XLA Ops:
  0.0 1.1 %copy-start = (f32[4,6,2,32,128]{4,3,2,1,0:T(8,128)S(1)}, f32[4,6,2,32,128]{4,3,2,1,0:T(8,128)}, u32[]{:S(2)}) copy-start(f32[4,6,2,32,128]{4,3,2,1,0:T(8,128)} %flow.1) | copy-start | bytes 2359300
  1.1 0.9 %copy-start.1 = (f32[11,2,8,128]{3,2,1,0:T(8,128)S(1)}, f32[11,2,8,128]{3,2,1,0:T(8,128)}, u32[]{:S(2)}) copy-start(f32[11,2,8,128]{3,2,1,0:T(8,128)} %metrics.1) | copy-start | bytes 270340

commit v2 on v1

--- a/solution.py
+++ b/solution.py
@@ -11,6 +11,7 @@
 GROUPS = 4
 PER = 4
 TILES = 12
+LAG = 6
 GAMMA = 1.4
 EPS_TWO = 0.1
 EPS_FOUR = 0.03125
@@ -99,7 +100,7 @@
     return a[0] * b[0] + a[1] * b[1] + a[2] * b[2]
 
 
-def face(wm, wl, wr, wp, pl_, pr_, geo, scaled=None):
+def face(wl, wr, outer, pl_, pr_, geo, scaled=None):
     hs, length, cond = geo[0:3], geo[3], geo[4]
     ql = dot3(pl_["u"], hs)
     qr = dot3(pr_["u"], hs)
@@ -122,7 +123,7 @@
         if f == 5:
             c = c - g * (pr_["n"] - pl_["n"])
         d = wr[f] - wl[f]
-        out.append(c - scaled * (JUMP_RATIO * d - (wp[f] - wm[f])))
+        out.append(c - scaled * (JUMP_RATIO * d - outer(f)))
     return out, rad, scaled
 
 
@@ -279,35 +280,42 @@
         for p in range(2):
             w = [w_of(f, p) for f in range(6)]
             prim = primitives(w)
-            yu, yuu, yd, zu, zuu, zd, zdd = [], [], [], [], [], [], []
+
+            up = [y_up(m, w[f], lane_roll(w[f], -32), 1) for f in range(6)]
+            flux, rad, sc = face(
+                w, up,
+                lambda f: y_up(m, w[f], lane_roll(w[f], -32), 2) - y_down(m, w[f], 1),
+                prim, primitives(up), [gy[p, c] for c in range(5)], None if first else ry[i, p],
+            )
+            total = [flux[f] - y_down(m, flux[f], 1) for f in range(6)]
+            total[5] = total[5] + mt[16 * p + 15] * w[5] * w[5] / w[0]
+            if first:
+                ry[i, p] = sc
+                radii = rad + y_down(m, rad, 1) + 8.0 * mt[16 * p + 3]
+
+            above = [lane_roll(high_pack, 32 - 2 * (2 * f + p)) for f in range(6)]
+            below = [lane_roll(low_pack, -2 - 2 * (2 * f + p)) for f in range(6)]
+            up = [lane_roll(jnp.where(m.zlo == 0, above[f], w[f]), -1) for f in range(6)]
+            down = [lane_roll(jnp.where(m.zlo == 31, below[f], w[f]), 1) for f in range(6)]
+            flux, rad, sc = face(
+                w, up,
+                lambda f: lane_roll(jnp.where(m.zlo < 2, above[f], w[f]), -2) - down[f],
+                prim, primitives(up), [gz[p, 0, c] for c in range(5)], None if first else rz[i, p, 0],
+            )
+            total = [total[f] + flux[f] for f in range(6)]
+            if first:
+                rz[i, p, 0] = sc
+                radii = radii + rad
+            flux, rad, sc = face(
+                down, w,
+                lambda f: up[f] - lane_roll(jnp.where(m.zlo >= 30, below[f], w[f]), 2),
+                primitives(down), prim, [gz[p, 1, c] for c in range(5)], None if first else rz[i, p, 1],
+            )
+            if first:
+                rz[i, p, 1] = sc
+                den[i, p] = radii + rad
             for f in range(6):
-                k = 2 * f + p
-                w32 = lane_roll(w[f], -32)
-                yu.append(y_up(m, w[f], w32, 1))
-                yuu.append(y_up(m, w[f], w32, 2))
-                yd.append(y_down(m, w[f], 1))
-                hi = lane_roll(high_pack, 32 - 2 * k)
-                lo = lane_roll(low_pack, -2 - 2 * k)
-                zu.append(lane_roll(jnp.where(m.zlo == 0, hi, w[f]), -1))
-                zuu.append(lane_roll(jnp.where(m.zlo < 2, hi, w[f]), -2))
-                zd.append(lane_roll(jnp.where(m.zlo == 31, lo, w[f]), 1))
-                zdd.append(lane_roll(jnp.where(m.zlo >= 30, lo, w[f]), 2))
-            geo_y = [gy[p, c] for c in range(5)]
-            geo_z = [gz[p, 0, c] for c in range(5)]
-            geo_l = [gz[p, 1, c] for c in range(5)]
-            known = (None, None, None) if first else (ry[i, p], rz[i, p, 0], rz[i, p, 1])
-            fy, rad_y, sc_y = face(yd, w, yu, yuu, prim, primitives(yu), geo_y, known[0])
-            fz, rad_z, sc_z = face(zd, w, zu, zuu, prim, primitives(zu), geo_z, known[1])
-            fl, rad_l, sc_l = face(zdd, zd, w, zu, primitives(zd), prim, geo_l, known[2])
-            if first:
-                ry[i, p] = sc_y
-                rz[i, p, 0] = sc_z
-                rz[i, p, 1] = sc_l
-                den[i, p] = rad_y + y_down(m, rad_y, 1) + rad_z + rad_l + 8.0 * mt[16 * p + 3]
-            for f in range(6):
-                r = fy[f] - y_down(m, fy[f], 1) + fz[f] - fl[f]
-                if f == 5:
-                    r = r + mt[16 * p + 15] * w[5] * w[5] / w[0]
+                r = total[f] - flux[f]
                 if not first:
                     r = r + res[i, 2 * f + p]
                 res[i, 2 * f + p] = r
@@ -348,90 +356,109 @@
         for k in range(3):
             geo = [gx[k, c] for c in range(5)]
             fx, rad, sc = face(
-                planes[k], planes[k + 1], planes[k + 2], planes[k + 3],
+                planes[k + 1], planes[k + 2], lambda f, k=k: planes[k + 3][f] - planes[k][f],
                 prims[k], prims[k + 1], geo, None if first else rx[i, k],
             )
             if first:
                 rx[i, k] = sc
             fluxes.append(fx)
             radii.append(rad)
-        result = []
-        for p in range(2):
-            if first:
-                h = 0.5 / (den[i, p] + radii[p] + radii[p + 1])
-                step[i, p] = h
-            else:
-                h = step[i, p]
-            result.append([h * (res[i, 2 * f + p] + (fluxes[p + 1][f] - fluxes[p][f])) for f in range(6)])
-        return result
-
-    @pl.loop(0, NINST)
-    def _(n):
+        if first:
+            for p in range(2):
+                step[i, p] = 0.5 / (den[i, p] + radii[p] + radii[p + 1])
+        return [[fluxes[p + 1][f] - fluxes[p][f] for f in range(6)] for p in range(2)]
+
+    def arrival_order(n):
+        far = jnp.maximum(n - PER, 0)
         own = n < PER
-        far = jnp.maximum(n - PER, 0)
         j = jnp.where(own, n, far // 3)
         back = jnp.where(own, 0, lax.rem(far, 3) + 1)
-        i = lax.rem(t + nt - back, nt) * PER + j
-
-        @pl.when(own)
-        def _():
-            own_copy(j).wait()
-
-        @pl.when(n >= PER)
-        def _():
-            xin_arrival(back, j).wait_recv()
-            for c in forward(region.at[i, pl.ds(0, TILES)], i):
-                c.start()
-
-        cross(i, lambda f, p: region[i, 2 * f + p], region[i, TILES], region[i, TILES + 1], True)
-
-    mix(lambda i, q: region[i, q], True)
-
-    for c in plane_metrics:
-        c.wait_recv()
-    sx = [[mleft[c] for c in range(3)], [mt[c] for c in range(3)], [mt[16 + c] for c in range(3)]]
-    vx = [mleft[3], mt[3], mt[19], mright[0]]
-    for k in range(3):
-        for c, g in enumerate(geometry(sx[k], vx[k], vx[k + 1])):
-            gx[k, c] = g
-
-    def order(n):
-        return group(lax.rem(n, 4)) * PER + n // 4
-
-    def edge_copies(i):
+        return j, lax.rem(t + nt - back, nt) * PER + j
+
+    def block_order(n):
+        return n // 4, lax.rem(t + nt - lax.rem(n, 4), nt) * PER + n // 4
+
+    def plane_copies(i):
         return (
             remote(w1.at[i], hl1.at[i], wp_s.at[0, i], wp_r.at[0, i], right),
             remote(w1.at[i], hr1.at[i], wp_s.at[1, i], wp_r.at[1, i], left),
+        )
+
+    def column_copies(i):
+        return (
             remote(zs.at[i, 0], z1.at[i, 1], z_s.at[0, i], z_r.at[0, i], (group(3), s)),
             remote(zs.at[i, 1], z1.at[i, 0], z_s.at[1, i], z_r.at[1, i], (group(1), s)),
         )
 
-    @pl.loop(0, NINST)
+    def receive_block(j):
+        sources = [(k, lax.rem(t + nt - k, nt) * PER + j) for k in (1, 3, 2)]
+        for k, i in sources:
+            xin_arrival(k, j).wait_recv()
+            for c in forward(region.at[i, pl.ds(0, TILES)], i):
+                c.start()
+
+    def face_metrics():
+        for c in plane_metrics:
+            c.wait_recv()
+        sx = [[mleft[c] for c in range(3)], [mt[c] for c in range(3)], [mt[16 + c] for c in range(3)]]
+        vx = [mleft[3], mt[3], mt[19], mright[0]]
+        for k in range(3):
+            for c, g in enumerate(geometry(sx[k], vx[k], vx[k + 1])):
+                gx[k, c] = g
+
+    @pl.loop(0, 2 * NINST)
     def _(n):
-        i = order(n)
-        for c in forward(region.at[i, pl.ds(0, TILES)], i):
-            c.wait_recv()
-        change = axial(i, lambda f, p: region[i, 2 * f + p], hl0, hr0, True)
-        low = high = None
-        for q in range(TILES):
-            f, p = divmod(q, 2)
-            v = region[i, q] - 0.5 * change[p][f]
-            w1[i, q] = v
-            low = pack_edge(m, low, v, q, 0)
-            high = pack_edge(m, high, v, q, 30)
-        zs[i, 0] = low
-        zs[i, 1] = high
-        for c in edge_copies(i):
-            c.start()
+        k = n - NINST
+
+        @pl.when(n < NINST)
+        def _():
+            j, i = arrival_order(n)
+
+            @pl.when(n < PER)
+            def _():
+                own_copy(j).wait()
+
+            @pl.when((n >= PER) & (lax.rem(jnp.maximum(n - PER, 0), 3) == 0))
+            def _():
+                receive_block(j)
+
+            cross(i, lambda f, p: region[i, 2 * f + p], region[i, TILES], region[i, TILES + 1], True)
+
+        @pl.when(n == LAG)
+        def _():
+            face_metrics()
+
+        @pl.when(k == 0)
+        def _():
+            mix(lambda i, q: region[i, q], True)
+
+        late = (k >= 2 * PER) & (lax.rem(n, 4) != 0)
+
+        @pl.when(((n >= LAG) & (n < NINST)) | late)
+        def _():
+            i = jnp.where(n < NINST, arrival_order(n - LAG)[1], block_order(jnp.maximum(k, 0))[1])
+            for c in forward(region.at[i, pl.ds(0, TILES)], i):
+                c.wait_recv()
+            change = axial(i, lambda f, p: region[i, 2 * f + p], hl0, hr0, True)
+            for p in range(2):
+                for f in range(6):
+                    res[i, 2 * f + p] = res[i, 2 * f + p] + change[p][f]
+
+        @pl.when(k >= 0)
+        def _():
+            j, i = block_order(jnp.maximum(k, 0))
+            low = high = None
+            for q in range(TILES):
+                v = region[i, q] - 0.5 * step[i, q % 2] * res[i, q]
+                w1[i, q] = v
+                low = pack_edge(m, low, v, q, 0)
+                high = pack_edge(m, high, v, q, 30)
+            zs[i, 0] = low
+            zs[i, 1] = high
+            for c in plane_copies(i) + column_copies(i):
+                c.start()
 
     mix(lambda i, q: w1[i, q], False)
-
-    @pl.loop(0, NINST)
-    def _(n):
-        i = order(n)
-        for c in edge_copies(i)[2:]:
-            c.wait_recv()
-        cross(i, lambda f, p: w1[i, 2 * f + p], z1[i, 0], z1[i, 1], False)
 
     def out_copy(k, j):
         g = group(k)
@@ -448,27 +475,28 @@
     def store_out(j):
         return pltpu.make_async_copy(ov.at[j], out.at[j], out_sem.at[j])
 
-    @pl.loop(0, PER)
-    def _(j):
-        @pl.loop(0, 4)
-        def _(k):
-            g = group(k)
-            i = g * PER + j
-            for c in edge_copies(i)[:2]:
-                c.wait_recv()
-            change = axial(i, lambda f, p: w1[i, 2 * f + p], hl1, hr1, False)
+    @pl.loop(0, NINST)
+    def _(n):
+        j, i = block_order(n)
+        back = lax.rem(n, 4)
+        for c in column_copies(i):
+            c.wait_recv()
+        cross(i, lambda f, p: w1[i, 2 * f + p], z1[i, 0], z1[i, 1], False)
+        for c in plane_copies(i):
+            c.wait_recv()
+        change = axial(i, lambda f, p: w1[i, 2 * f + p], hl1, hr1, False)
+        for p in range(2):
+            for f in range(6):
+                ob[i, 2 * f + p] = -step[i, p] * (res[i, 2 * f + p] + change[p][f])
+
+        @pl.when(back > 0)
+        def _():
+            out_copy(4 - back, j).start()
+
+        @pl.when(back == 0)
+        def _():
             for q in range(TILES):
-                f, p = divmod(q, 2)
-                ob[i, q] = -change[p][f]
-
-            @pl.when(k > 0)
-            def _():
-                out_copy(k, j).start()
-
-            @pl.when(k == 0)
-            def _():
-                for q in range(TILES):
-                    oin[t, j, q] = ob[i, q]
+                oin[t, j, q] = ob[i, q]
 
     @pl.loop(0, PER)
     def _(j):
@@ -496,7 +524,7 @@
     def _(i):
         for c in forward(region.at[i, pl.ds(0, TILES)], i):
             c.wait_send()
-        for c in edge_copies(i):
+        for c in plane_copies(i) + column_copies(i):
             c.wait_send()
 
     for j in range(PER):
@@ -565,7 +593,7 @@
             dma((3, PER)),
         ],
         compiler_params=pltpu.CompilerParams(
-            collective_id=0, has_side_effects=True, vmem_limit_bytes=32 << 20
+            collective_id=0, has_side_effects=True, vmem_limit_bytes=53 << 20
         ),
         cost_estimate=pl.CostEstimate(
             flops=100_000_000, bytes_accessed=1_800_000, transcendentals=200_000

time: 43.4 us -> 42.3 us (0.975)
  local copies, waits for them, and re-layouts: 2.9 us -> 1.77 us
    unnamed x5 -> x3, local copies, waits for them, and re-layouts: 2.9 us -> 1.77 us
where the time goes in v2:
time: 42.3 us; the launch traced here: 42.1 us
  Pallas kernels  40.4 us (96%)
  local copies, waits for them, and re-layouts  1.77 us (4%)
    pallas_call x1, Pallas kernels, per_device(): pl.pallas_call(kernel, out_shape=jax.ShapeDtypeStruct(flow_state.shape, f...  40.4 us
    unnamed x3, local copies, waits for them, and re-layouts  1.77 us

profile of v2, /device:TPU:2, one launch (start us, length us, event | category | flops | bytes accessed | tf_op | source)
XLA Modules:
  0.0 42.1 jit_solution(8827127415705206019)
XLA Ops:
  0.0 0.0 copy-start
  0.0 0.9 %copy-done = f32[11,2,8,128]{3,2,1,0:T(8,128)S(1)} copy-done((f32[11,2,8,128]{3,2,1,0:T(8,128)S(1)}, f32[11,2,8,128]{3,2,1,0:T(8,128)}, u32[]{:S(2)}) %copy-start) | copy-done | bytes 90136
  0.9 40.4 %balance.1 = f32[4,6,2,32,128]{4,3,2,1,0:T(8,128)S(1)} custom-call(f32[4,6,2,32,128]{4,3,2,1,0:T(8,128)} %flow.1, f32[11,2,8,128]{3,2,1,0:T(8,128)S(1)} %copy-done), custom_call_target="tpu_custom_call" | custom-call | flops 100000000 | bytes 1800000 | tf_op jit(solution)/shard_map/balance/pallas_call | solution.py:543
  41.3 0.9 %copy.4 = f32[4,6,2,32,128]{4,3,2,1,0:T(8,128)} copy(f32[4,6,2,32,128]{4,3,2,1,0:T(8,128)S(1)} %balance.1) | data formatting | bytes 1572864
Async XLA Ops:
  0.0 0.9 %copy-start = (f32[11,2,8,128]{3,2,1,0:T(8,128)S(1)}, f32[11,2,8,128]{3,2,1,0:T(8,128)}, u32[]{:S(2)}) copy-start(f32[11,2,8,128]{3,2,1,0:T(8,128)} %metrics.1) | copy-start | bytes 270340

commit v3 on v2

--- a/solution.py
+++ b/solution.py
@@ -11,7 +11,8 @@
 GROUPS = 4
 PER = 4
 TILES = 12
-LAG = 6
+LAG = 9
+AHEAD = 8
 GAMMA = 1.4
 EPS_TWO = 0.1
 EPS_FOUR = 0.03125
@@ -46,6 +47,7 @@
         lane = lax.broadcasted_iota(jnp.int32, (8, 128), 1)
         self.row = lax.broadcasted_iota(jnp.int32, (8, 128), 0)
         self.zlo = lane & 31
+        self.pair = self.zlo >> 1
         self.half = lane < 64
         self.even = (lane & 32) == 0
 
@@ -63,9 +65,10 @@
     ]
 
 
-def pack_edge(m, acc, tile, k, first):
-    moved = lane_roll(tile, 2 * k - first)
-    return moved if acc is None else jnp.where((m.zlo >> 1) == k, moved, acc)
+def pack_edges(m, low, high, moved, k):
+    low = moved if low is None else jnp.where(m.pair == k, moved, low)
+    high = moved if high is None else jnp.where(m.pair == (k - 1) % 16, moved, high)
+    return low, high
 
 
 def y_up(m, w, w32, k):
@@ -138,10 +141,10 @@
 
 def kernel(
     flow, metrics, out,
-    xv, mv, sbuf, region, hl0, hr0, res, w1, zs, z1, hl1, hr1, ob, oin, ov,
+    xv, mv, sbuf, region, hl0, hr0, res, coupling, w1, moved1, zs, z1, hl1, hr1, ob, oin, ov,
     ms, mr, mt, mleft, mright, gx, gy, gz, ry, rz, rx, den, step,
     in_sem, own_sem, out_sem, met_s, met_r, pm_s, pm_r,
-    xin_s, xin_r, fw_s, fw_r, wp_s, wp_r, z_s, z_r, o_s, o_r,
+    go, xin_s, xin_r, fw_s, fw_r, wp_s, wp_r, z_s, z_r, o_s, o_r,
 ):
     t = lax.axis_index("tm")
     s = lax.axis_index("space")
@@ -149,6 +152,7 @@
     ns = lax.axis_size("space")
     right = (t, lax.rem(s + 1, ns))
     left = (t, lax.rem(s + ns - 1, ns))
+    upper = lax.rem(s, 2) == 1
 
     def group(k):
         return lax.rem(t + k, nt)
@@ -206,11 +210,10 @@
             tiles = swap_segments(m, [xv[j, f, p, 8 * y : 8 * y + 8, :] for y in range(4)])
             for b in range(4):
                 sbuf[b, j, q] = tiles[b]
-                low[b] = pack_edge(m, low[b], tiles[b], q, 0)
-                high[b] = pack_edge(m, high[b], tiles[b], q, 30)
+                low[b], high[b] = pack_edges(m, low[b], high[b], lane_roll(tiles[b], 2 * q), q)
         for b in range(4):
-            sbuf[(b + 1) % 4, j, TILES] = high[b]
-            sbuf[(b + 3) % 4, j, TILES + 1] = low[b]
+            sbuf[(b + 1) % 4, j, TILES] = lane_roll(high[b], -32)
+            sbuf[(b + 3) % 4, j, TILES + 1] = lane_roll(low[b], 32)
 
     def met_copy(k):
         return remote(ms.at[group(k)], mr.at[t], met_s.at[k - 1], met_r.at[k - 1], (group(k), s))
@@ -247,11 +250,26 @@
     @pl.loop(0, PER)
     def _(j):
         pack(j)
-        for k in (2, 1, 3):
-            xin_copy(k, j).start()
+
+        @pl.when(upper)
+        def _():
+            for k in (2, 1, 3):
+                xin_copy(k, j).start()
+
         for c in forward(sbuf.at[t, j, pl.ds(0, TILES)], t * PER + j):
             c.start()
         own_copy(j).start()
+
+    @pl.when(upper)
+    def _():
+        pl.semaphore_signal(go, inc=1, device_id=left, device_id_type=MESH)
+
+    @pl.when(jnp.logical_not(upper))
+    def _():
+        pl.semaphore_wait(go, 1)
+        for j in range(PER):
+            for k in (2, 1, 3):
+                xin_copy(k, j).start()
 
     for k in (2, 1, 3):
         met_arrival(k).wait_recv()
@@ -276,7 +294,7 @@
             gz[p, 0, c] = geo_z[c]
             gz[p, 1, c] = geo_l[c]
 
-    def cross(i, w_of, low_pack, high_pack, first):
+    def cross(i, w_of, moved_of, low_pack, high_pack, first):
         for p in range(2):
             w = [w_of(f, p) for f in range(6)]
             prim = primitives(w)
@@ -293,13 +311,17 @@
                 ry[i, p] = sc
                 radii = rad + y_down(m, rad, 1) + 8.0 * mt[16 * p + 3]
 
-            above = [lane_roll(high_pack, 32 - 2 * (2 * f + p)) for f in range(6)]
-            below = [lane_roll(low_pack, -2 - 2 * (2 * f + p)) for f in range(6)]
-            up = [lane_roll(jnp.where(m.zlo == 0, above[f], w[f]), -1) for f in range(6)]
-            down = [lane_roll(jnp.where(m.zlo == 31, below[f], w[f]), 1) for f in range(6)]
+            moved = [moved_of(f, p) for f in range(6)]
+            at = [2 * f + p for f in range(6)]
+
+            def shifted(f, mask, pack, k):
+                return lane_roll(jnp.where(mask, pack, moved[f]), k - 2 * at[f])
+
+            up = [shifted(f, m.zlo == 2 * at[f], high_pack, -1) for f in range(6)]
+            down = [shifted(f, m.zlo == (2 * at[f] - 1) % 32, low_pack, 1) for f in range(6)]
             flux, rad, sc = face(
                 w, up,
-                lambda f: lane_roll(jnp.where(m.zlo < 2, above[f], w[f]), -2) - down[f],
+                lambda f: shifted(f, m.pair == at[f], high_pack, -2) - down[f],
                 prim, primitives(up), [gz[p, 0, c] for c in range(5)], None if first else rz[i, p, 0],
             )
             total = [total[f] + flux[f] for f in range(6)]
@@ -308,17 +330,14 @@
                 radii = radii + rad
             flux, rad, sc = face(
                 down, w,
-                lambda f: up[f] - lane_roll(jnp.where(m.zlo >= 30, below[f], w[f]), 2),
+                lambda f: up[f] - shifted(f, m.pair == (at[f] - 1) % 16, low_pack, 2),
                 primitives(down), prim, [gz[p, 1, c] for c in range(5)], None if first else rz[i, p, 1],
             )
             if first:
                 rz[i, p, 1] = sc
                 den[i, p] = radii + rad
             for f in range(6):
-                r = total[f] - flux[f]
-                if not first:
-                    r = r + res[i, 2 * f + p]
-                res[i, 2 * f + p] = r
+                res[i, 2 * f + p] = total[f] - flux[f]
 
     def mix(w_of, first):
         pc = [0.5 * (table_entry(d) + table_entry(d - 8)) for d in range(5)]
@@ -340,7 +359,10 @@
                     odd = odd + qc[d] * (a[(r - d) % 16] - a[(r + d) % 16])
                 for i, v in ((r, even + odd), (r + 8, even - odd)):
                     v = vol * v
-                    res[i, q] = res[i, q] + v if first else v
+                    if first:
+                        res[i, q] = res[i, q] + v
+                    else:
+                        coupling[i, q] = v
 
     def axial(i, w_of, hl, hr, first):
         planes = [
@@ -406,6 +428,16 @@
             for c, g in enumerate(geometry(sx[k], vx[k], vx[k + 1])):
                 gx[k, c] = g
 
+    def second_cross(i):
+        for c in column_copies(i):
+            c.wait_recv()
+        cross(
+            i,
+            lambda f, p: w1[i, 2 * f + p],
+            lambda f, p: moved1[i, 2 * f + p],
+            z1[i, 0], z1[i, 1], False,
+        )
+
     @pl.loop(0, 2 * NINST)
     def _(n):
         k = n - NINST
@@ -422,7 +454,12 @@
             def _():
                 receive_block(j)
 
-            cross(i, lambda f, p: region[i, 2 * f + p], region[i, TILES], region[i, TILES + 1], True)
+            cross(
+                i,
+                lambda f, p: region[i, 2 * f + p],
+                lambda f, p: lane_roll(region[i, 2 * f + p], 2 * (2 * f + p)),
+                region[i, TILES], region[i, TILES + 1], True,
+            )
 
         @pl.when(n == LAG)
         def _():
@@ -432,7 +469,11 @@
         def _():
             mix(lambda i, q: region[i, q], True)
 
-        late = (k >= 2 * PER) & (lax.rem(n, 4) != 0)
+        @pl.when(k >= AHEAD)
+        def _():
+            second_cross(block_order(jnp.maximum(k - AHEAD, 0))[1])
+
+        late = (k >= PER) & (lax.rem(n, 4) != 0)
 
         @pl.when(((n >= LAG) & (n < NINST)) | late)
         def _():
@@ -451,10 +492,11 @@
             for q in range(TILES):
                 v = region[i, q] - 0.5 * step[i, q % 2] * res[i, q]
                 w1[i, q] = v
-                low = pack_edge(m, low, v, q, 0)
-                high = pack_edge(m, high, v, q, 30)
-            zs[i, 0] = low
-            zs[i, 1] = high
+                moved = lane_roll(v, 2 * q)
+                moved1[i, q] = moved
+                low, high = pack_edges(m, low, high, moved, q)
+            zs[i, 0] = lane_roll(low, 32)
+            zs[i, 1] = lane_roll(high, -32)
             for c in plane_copies(i) + column_copies(i):
                 c.start()
 
@@ -479,15 +521,17 @@
     def _(n):
         j, i = block_order(n)
         back = lax.rem(n, 4)
-        for c in column_copies(i):
-            c.wait_recv()
-        cross(i, lambda f, p: w1[i, 2 * f + p], z1[i, 0], z1[i, 1], False)
+
+        @pl.when(n >= NINST - AHEAD)
+        def _():
+            second_cross(i)
+
         for c in plane_copies(i):
             c.wait_recv()
         change = axial(i, lambda f, p: w1[i, 2 * f + p], hl1, hr1, False)
         for p in range(2):
             for f in range(6):
-                ob[i, 2 * f + p] = -step[i, p] * (res[i, 2 * f + p] + change[p][f])
+                ob[i, 2 * f + p] = -step[i, p] * (res[i, 2 * f + p] + coupling[i, 2 * f + p] + change[p][f])
 
         @pl.when(back > 0)
         def _():
@@ -550,6 +594,8 @@
             pltpu.VMEM(metrics.shape, f32),
             vmem(GROUPS, PER, TILES + 2),
             vmem(NINST, TILES + 2),
+            vmem(*full),
+            vmem(*full),
             vmem(*full),
             vmem(*full),
             vmem(*full),
@@ -581,6 +627,7 @@
             dma((3,)),
             dma((2,)),
             dma((2,)),
+            pltpu.SemaphoreType.REGULAR,
             dma((3, PER)),
             dma((3, PER)),
             dma((2, NINST)),

time: 42.3 us -> 42 us (level)
  no operation moved by 1% of the time
where the time goes in v3:
time: 42 us; the launch traced here: 41.8 us
  Pallas kernels  40.1 us (95%)
  local copies, waits for them, and re-layouts  1.77 us (4%)
    pallas_call x1, Pallas kernels, per_device(): pl.pallas_call(kernel, out_shape=jax.ShapeDtypeStruct(flow_state.shape, f...  40.1 us
    unnamed x3, local copies, waits for them, and re-layouts  1.77 us

profile of v3, /device:TPU:2, one launch (start us, length us, event | category | flops | bytes accessed | tf_op | source)
XLA Modules:
  0.0 41.8 jit_solution(13107223836695196139)
XLA Ops:
  0.0 0.0 copy-start
  0.0 0.9 %copy-done = f32[11,2,8,128]{3,2,1,0:T(8,128)S(1)} copy-done((f32[11,2,8,128]{3,2,1,0:T(8,128)S(1)}, f32[11,2,8,128]{3,2,1,0:T(8,128)}, u32[]{:S(2)}) %copy-start) | copy-done | bytes 90136
  0.9 40.1 %balance.1 = f32[4,6,2,32,128]{4,3,2,1,0:T(8,128)S(1)} custom-call(f32[4,6,2,32,128]{4,3,2,1,0:T(8,128)} %flow.1, f32[11,2,8,128]{3,2,1,0:T(8,128)S(1)} %copy-done), custom_call_target="tpu_custom_call" | custom-call | flops 100000000 | bytes 1800000 | tf_op jit(solution)/shard_map/balance/pallas_call | solution.py:587
  41.0 0.9 %copy.4 = f32[4,6,2,32,128]{4,3,2,1,0:T(8,128)} copy(f32[4,6,2,32,128]{4,3,2,1,0:T(8,128)S(1)} %balance.1) | data formatting | bytes 1572864
Async XLA Ops:
  0.0 0.9 %copy-start = (f32[11,2,8,128]{3,2,1,0:T(8,128)S(1)}, f32[11,2,8,128]{3,2,1,0:T(8,128)}, u32[]{:S(2)}) copy-start(f32[11,2,8,128]{3,2,1,0:T(8,128)} %metrics.1) | copy-start | bytes 270340

commit v4 on v3

--- a/solution.py
+++ b/solution.py
@@ -542,6 +542,23 @@
             for q in range(TILES):
                 oin[t, j, q] = ob[i, q]
 
+    for k in (1, 2, 3):
+        met_copy(k).wait_send()
+    for c in plane_metrics:
+        c.wait_send()
+
+    @pl.loop(0, PER)
+    def _(j):
+        for k in (1, 2, 3):
+            xin_copy(k, j).wait_send()
+
+    @pl.loop(0, NINST)
+    def _(i):
+        for c in forward(region.at[i, pl.ds(0, TILES)], i):
+            c.wait_send()
+        for c in plane_copies(i) + column_copies(i):
+            c.wait_send()
+
     @pl.loop(0, PER)
     def _(j):
         for k in range(1, 4):
@@ -553,23 +570,10 @@
                 ov[j, f, p, 8 * y : 8 * y + 8, :] = tiles[y]
         store_out(j).start()
 
-    for k in (1, 2, 3):
-        met_copy(k).wait_send()
-    for c in plane_metrics:
-        c.wait_send()
-
     @pl.loop(0, PER)
     def _(j):
         for k in (1, 2, 3):
-            xin_copy(k, j).wait_send()
             out_copy(k, j).wait_send()
-
-    @pl.loop(0, NINST)
-    def _(i):
-        for c in forward(region.at[i, pl.ds(0, TILES)], i):
-            c.wait_send()
-        for c in plane_copies(i) + column_copies(i):
-            c.wait_send()
 
     for j in range(PER):
         store_out(j).wait()

time: 42 us -> 41.8 us (level)
  no operation moved by 1% of the time
where the time goes in v4:
time: 41.8 us; the launch traced here: 41.6 us
  Pallas kernels  39.9 us (95%)
  local copies, waits for them, and re-layouts  1.77 us (4%)
    pallas_call x1, Pallas kernels, per_device(): pl.pallas_call(kernel, out_shape=jax.ShapeDtypeStruct(flow_state.shape, f...  39.9 us
    unnamed x3, local copies, waits for them, and re-layouts  1.77 us

profile of v4, /device:TPU:2, one launch (start us, length us, event | category | flops | bytes accessed | tf_op | source)
XLA Modules:
  0.0 41.6 jit_solution(4273038844177174104)
XLA Ops:
  0.0 0.0 copy-start
  0.0 0.9 %copy-done = f32[11,2,8,128]{3,2,1,0:T(8,128)S(1)} copy-done((f32[11,2,8,128]{3,2,1,0:T(8,128)S(1)}, f32[11,2,8,128]{3,2,1,0:T(8,128)}, u32[]{:S(2)}) %copy-start) | copy-done | bytes 90136
  0.9 39.9 %balance.1 = f32[4,6,2,32,128]{4,3,2,1,0:T(8,128)S(1)} custom-call(f32[4,6,2,32,128]{4,3,2,1,0:T(8,128)} %flow.1, f32[11,2,8,128]{3,2,1,0:T(8,128)S(1)} %copy-done), custom_call_target="tpu_custom_call" | custom-call | flops 100000000 | bytes 1800000 | tf_op jit(solution)/shard_map/balance/pallas_call | solution.py:591
  40.8 0.9 %copy.4 = f32[4,6,2,32,128]{4,3,2,1,0:T(8,128)} copy(f32[4,6,2,32,128]{4,3,2,1,0:T(8,128)S(1)} %balance.1) | data formatting | bytes 1572864
Async XLA Ops:
  0.0 0.9 %copy-start = (f32[11,2,8,128]{3,2,1,0:T(8,128)S(1)}, f32[11,2,8,128]{3,2,1,0:T(8,128)}, u32[]{:S(2)}) copy-start(f32[11,2,8,128]{3,2,1,0:T(8,128)} %metrics.1) | copy-start | bytes 270340
